TPU v7x, 128 devices: a whole 4x4x4 slice. The times are simulated.
128 devices in a mesh: inp: 32 (over z_lo, x, y), tim: 4 (over z_hi, core).
Axes of the slice: x: 4, y: 4, z: 4 (z_hi: 2, z_lo: 2; z = z_hi * 2 + z_lo), core: 2. Of those that a mesh axis runs over, the one named last changes fastest.
Arguments:
- voltages: bfloat16 [1024, 524288], P('inp', 'tim'), may hold values from -6 to 6
Outputs:
- visibility: float32 [256, 2, 1024, 1024], P(('inp', 'tim'))
All inputs are finite; a program needn't handle non-finite values.
Results may differ from a plain program's by a relative error of at most 0.0063.
Values may be sent and summed in bfloat16 or wider, within the bound.
A program may use at most 128 MiB of HBM per device.

v0:
```python
import math

import jax
import jax.numpy as jnp
from jax import lax
from jax.sharding import PartitionSpec as P

NFFT = 2048
TAPS = 4
CH0 = 384
CH_DEV = 2


def shifted(array, axis, by):
    peers = lax.axis_size(axis)
    pairs = [(i, i + by) for i in range(peers) if 0 <= i + by < peers]
    return lax.ppermute(array, axis, pairs)


def filter_window(length, taps):
    places = jnp.arange(taps * length).astype(jnp.float32)
    span_total = taps * length
    centred = (places - span_total / 2 + 0.5) / length
    taper = 0.5 - 0.5 * jnp.cos(2.0 * math.pi * (places + 0.5) / span_total)
    return (jnp.sinc(centred) * taper).reshape(taps, length)


def device_table(length, first, device_count, per_device):
    owners = jnp.arange(device_count)
    within = jnp.arange(per_device)
    channels = (first + owners[:, None] * per_device + within[None, :]).reshape(
        device_count, 1, per_device
    )
    samples = jnp.arange(length)
    phase = channels[:, :, :, None] * samples[None, None, None, :] % length
    angle = phase.astype(jnp.float32) * (2.0 * math.pi / length)
    scaling = 1.0 / math.sqrt(length)
    both = jnp.concatenate([jnp.cos(angle) * scaling, -jnp.sin(angle) * scaling], axis=1)
    return both.reshape(device_count * 2 * per_device, length).astype(jnp.bfloat16)


def local(voltages):
    local_inputs = voltages.shape[0]
    local_frames = voltages.shape[1] // NFFT
    inp_count = lax.axis_size("inp")
    tim_count = lax.axis_size("tim")
    device_count = inp_count * tim_count
    all_inputs = inp_count * local_inputs
    window = filter_window(NFFT, TAPS)
    table_rows = device_table(NFFT, CH0, device_count, CH_DEV)
    leading = voltages[:, : (TAPS - 1) * NFFT]
    trailing = shifted(leading, "tim", -1)
    stream = jnp.concatenate([voltages, trailing], axis=1).reshape(
        local_inputs, local_frames + TAPS - 1, NFFT
    )
    summed = jnp.zeros((local_inputs, local_frames, NFFT), jnp.float32)
    for tap_index in range(TAPS):
        summed = summed + window[tap_index][None, None, :] * stream[
            :, tap_index : tap_index + local_frames, :
        ].astype(jnp.float32)
    filtered = summed.astype(jnp.bfloat16).reshape(local_inputs * local_frames, NFFT)
    spectra = lax.dot_general(
        table_rows, filtered, (((1,), (1,)), ((), ())), preferred_element_type=jnp.float32
    )
    spectra = spectra.astype(jnp.bfloat16)
    scale = 1.0 / (local_frames * tim_count)
    outgoing = spectra.reshape(device_count, 2, CH_DEV, local_inputs, local_frames)
    turned = lax.all_to_all(outgoing, ("inp", "tim"), split_axis=0, concat_axis=0, tiled=True)
    turned = turned.reshape(inp_count, tim_count, 2, CH_DEV, local_inputs, local_frames)
    turned = jnp.transpose(turned, (2, 3, 1, 0, 4, 5)).reshape(
        2, CH_DEV, tim_count, all_inputs, local_frames
    )
    form = "ctik,ctjk->cij"
    real_part = turned[0]
    imag_part = turned[1]
    real_real = jnp.einsum(form, real_part, real_part, preferred_element_type=jnp.float32)
    imag_imag = jnp.einsum(form, imag_part, imag_part, preferred_element_type=jnp.float32)
    imag_real = jnp.einsum(form, imag_part, real_part, preferred_element_type=jnp.float32)
    real_imag = jnp.einsum(form, real_part, imag_part, preferred_element_type=jnp.float32)
    visibility = jnp.stack(
        [(real_real + imag_imag) * scale, (imag_real - real_imag) * scale], axis=1
    )
    return visibility


def solution(mesh):
    placed = (P("inp", "tim"),)
    return jax.shard_map(
        local,
        mesh=mesh,
        in_specs=placed,
        out_specs=P(("inp", "tim"), None, None, None),
        check_vma=False,
    )
```

profile of v0, /device:TPU:1, one launch (start us, length us, event | category | flops | bytes accessed | tf_op | source)
XLA Modules:
  0.0 154.8 jit_solution(10103291186958897881)
XLA Ops:
  0.0 1.0 slice.40
  1.0 3.3 %collective-permute-start = (bf16[32,6144]{1,0:T(8,128)(2,1)S(1)}, bf16[32,6144]{1,0:T(8,128)(2,1)S(1)}, u32[]{:S(2)}, u32[]{:S(2)}) collective-permute-start(bf16[32,6144]{1,0:T(8,128)(2,1)S(1)} %slice.40), channel_id=1, source_target_pairs={{1,0},{2,1},{3,2},{5,4},{6,5},{7,6},{9,8},{10,9},{11,10},{13,12},{... | collective-permute-start | bytes 1179656 | tf_op jit(solution)/shard_map/ppermute | solution.py:17
  4.4 9.1 %multiply_convert_fusion.1 = (bf16[128,1,2,2048]{3,0,2,1:T(8,128)(2,1)S(1)}, bf16[128,1,2,2048]{3,0,2,1:T(8,128)(2,1)S(1)}) fusion(s32[128,2]{0,1:T(2,128)S(1)} %iota_add_fusion), kind=kLoop, calls=%fused_computation.19 | loop fusion | flops 9961472 | bytes 2098176 | tf_op jit(solution)/shard_map/convert
  13.5 0.2 pad_maximum_fusion.2
  13.7 2.2 %copy.24 = bf16[128,2,2,2048]{3,2,1,0:T(2,128)(2,1)S(1)} copy(bf16[128,2,2,2048]{3,0,2,1:T(8,128)(2,1)S(1)} %pad_maximum_fusion.2) | data formatting | bytes 4194304 | tf_op jit(solution)/shard_map/concatenate | solution.py:38
  15.9 2.3 %convert_element_type.60 = bf16[512,2048]{1,0:T(8,128)(2,1)} reshape(bf16[128,2,2,2048]{3,2,1,0:T(2,128)(2,1)S(1)} %copy.24) | data formatting | bytes 4194304 | tf_op jit(solution)/shard_map/convert_element_type | solution.py:39
  18.2 0.2 fusion.14
  18.3 0.0 collective-permute-done
  18.4 11.5 %pad_maximum_fusion.1 = bf16[32,137216]{1,0:T(8,128)(2,1)} fusion(bf16[32,6144]{1,0:T(8,128)(2,1)S(1)} %collective-permute-done, bf16[32,131072]{1,0:T(8,128)(2,1)} %param.1), kind=kLoop, calls=%fused_computation.2 | loop fusion | flops 17563648 | bytes 17563648 | tf_op jit(solution)/shard_map/concatenate | solution.py:53
  29.9 9.5 %reshape.142 = bf16[32,67,2048]{2,1,0:T(8,128)(2,1)} reshape(bf16[32,137216]{1,0:T(8,128)(2,1)} %pad_maximum_fusion.1) | data formatting | bytes 17563648 | tf_op jit(solution)/shard_map/reshape | solution.py:53
  39.4 19.2 %add_convert_fusion = bf16[32,64,2048]{2,1,0:T(8,128)(2,1)S(1)} fusion(bf16[32,67,2048]{2,1,0:T(8,128)(2,1)} %reshape.142, f32[2048]{0:T(1024)S(1)} %get-tuple-element.8, f32[2048]{0:T(1024)S(1)} %get-tuple-element.9, f32[2048]{0:T(1024)S(1)} %get-tuple-element.10, f32[2048]{0:T(1024)S(1)} %get-tuple-element.7), kind=kLoop, calls=%fused_computation.1 | loop fusion | flops 50331648 | bytes 41975808 | tf_op jit(solution)/shard_map/convert_element_type | solution.py:61
  58.6 5.0 %convolution_convert_fusion = bf16[512,2048]{1,0:T(8,128)(2,1)S(1)} fusion(bf16[512,2048]{1,0:T(8,128)(2,1)S(1)} %copy-done.1, bf16[2048,2048]{1,0:T(8,128)(2,1)S(1)} %bitcast.49), kind=kOutput, calls=%fused_computation.13 | convolution fusion | flops 4296015872 | bytes 12582912 | tf_op jit(solution)/shard_map/dot_general | solution.py:62
  63.6 5.3 %reshape.144 = bf16[128,2,2,32,64]{4,3,2,1,0:T(8,128)(2,1)} reshape(bf16[512,2048]{1,0:T(8,128)(2,1)S(1)} %convolution_convert_fusion) | data formatting | bytes 4194304 | tf_op jit(solution)/shard_map/reshape | solution.py:67
  68.9 6.7 %reshape.150 = bf16[128,2,4096]{2,1,0:T(2,128)(2,1)S(1)} reshape(bf16[128,2,2,32,64]{4,3,2,1,0:T(8,128)(2,1)} %reshape.144) | data formatting | bytes 4194304
  75.6 40.1 %all_to_all.5 = bf16[128,2,4096]{2,1,0:T(2,128)(2,1)} all-to-all(bf16[128,2,4096]{2,1,0:T(2,128)(2,1)S(1)} %reshape.150), channel_id=1, replica_groups=mesh['inp'=32,'tim'=4] {'inp','tim'}, dimensions={0} | all-to-all | bytes 4194304 | tf_op jit(solution)/shard_map/all_to_all | solution.py:68
  115.7 7.8 %reshape.151 = bf16[128,2,2,32,64]{4,3,2,1,0:T(8,128)(2,1)} reshape(bf16[128,2,4096]{2,1,0:T(2,128)(2,1)} %all_to_all.5) | data formatting | bytes 4194304
  123.5 3.3 %copy.48 = bf16[32,4,2,2,32,64]{5,4,0,1,3,2:T(8,128)(2,1)S(1)} copy(bf16[32,4,2,2,32,64]{5,4,3,2,1,0:T(8,128)(2,1)} %bitcast.48) | data formatting | bytes 4194304 | tf_op jit(solution)/shard_map/reshape | solution.py:69
  126.8 0.7 fusion.23
  127.5 2.4 %fusion.25 = f32[2,1024,1024,1]{2,1,3,0:T(8,128)S(1)} fusion(bf16[2,4,1024,64]{3,2,1,0:T(8,128)(2,1)S(1)} %bitcast.44), kind=kOutput, calls=%fused_computation.51 | convolution fusion | flops 1073741824 | bytes 9437184 | tf_op jit(solution)/shard_map/ctik,ctjk->cij/dot_general | solution.py:76
  129.9 2.4 %fusion.26 = f32[2,1024,1024,1]{2,1,3,0:T(8,128)S(1)} fusion(bf16[2,4,1024,64]{3,2,1,0:T(8,128)(2,1)S(1)} %bitcast.41, bf16[2,4,1024,64]{3,2,1,0:T(8,128)(2,1)S(1)} %bitcast.45), kind=kOutput, calls=%fused_computation.52 | convolution fusion | flops 1073741824 | bytes 10485760 | tf_op jit(solution)/shard_map/ctik,ctjk->cij/dot_general | solution.py:78
  132.3 5.8 %fusion.1 = f32[2,1,1024,1024]{3,2,0,1:T(8,128)} fusion(f32[2,1024,1024,1]{2,1,3,0:T(8,128)S(1)} %fusion.26, bf16[2,4,1024,64]{3,2,1,0:T(8,128)(2,1)S(1)} %bitcast.46, bf16[2,4,1024,64]{3,2,1,0:T(8,128)(2,1)S(1)} %bitcast.42), kind=kOutput, calls=%fused_computation.5 | convolution fusion | flops 1077936128 | bytes 18874368 | tf_op jit(solution)/shard_map/ctik,ctjk->cij/dot_general | solution.py:79
  138.0 5.6 %fusion.3 = f32[2,1,1024,1024]{3,2,0,1:T(8,128)} fusion(f32[2,1024,1024,1]{2,1,3,0:T(8,128)S(1)} %fusion.25, bf16[2,4,1024,64]{3,2,1,0:T(8,128)(2,1)S(1)} %bitcast.43), kind=kOutput, calls=%fused_computation.8 | convolution fusion | flops 1077936128 | bytes 17825792 | tf_op jit(solution)/shard_map/ctik,ctjk->cij/dot_general | solution.py:77
  143.6 4.9 %pad_maximum_fusion = f32[2,2,1024,1024]{3,2,0,1:T(8,128)S(1)} fusion(f32[2,1,1024,1024]{3,2,0,1:T(8,128)S(1)} %copy-done, f32[2,1,1024,1024]{3,2,0,1:T(8,128)} %fusion.3), kind=kLoop, calls=%fused_computation | loop fusion | flops 4194304 | bytes 33554432 | tf_op jit(solution)/shard_map/stack | solution.py:80
  148.5 6.3 %copy.34 = f32[2,2,1024,1024]{3,2,1,0:T(8,128)} copy(f32[2,2,1024,1024]{3,2,0,1:T(8,128)S(1)} %pad_maximum_fusion) | data formatting | bytes 33554432 | tf_op jit(solution)/shard_map/stack | solution.py:80
  (7 shorter events, 0.0 us)
Async XLA Ops:
  1.0 17.3 %collective-permute-start = (bf16[32,6144]{1,0:T(8,128)(2,1)S(1)}, bf16[32,6144]{1,0:T(8,128)(2,1)S(1)}, u32[]{:S(2)}, u32[]{:S(2)}) collective-permute-start(bf16[32,6144]{1,0:T(8,128)(2,1)S(1)} %slice.40), channel_id=1, source_target_pairs={{1,0},{2,1},{3,2},{5,4},{6,5},{7,6},{9,8},{10,9},{11,10},{13,12},{... | collective-permute-start | bytes 1179656 | tf_op jit(solution)/shard_map/ppermute | solution.py:17
  39.4 19.2 %copy-start.1 = (bf16[512,2048]{1,0:T(8,128)(2,1)S(1)}, bf16[512,2048]{1,0:T(8,128)(2,1)}, u32[]{:S(2)}) copy-start(bf16[512,2048]{1,0:T(8,128)(2,1)} %convert_element_type.60) | copy-start | bytes 6291460
  138.0 5.6 %copy-start = (f32[2,1,1024,1024]{3,2,0,1:T(8,128)S(1)}, f32[2,1,1024,1024]{3,2,0,1:T(8,128)}, u32[]{:S(2)}) copy-start(f32[2,1,1024,1024]{3,2,0,1:T(8,128)} %fusion.1) | copy-start | bytes 25165828
where the time goes:
time: 155 us
  local copies, waits for them, and re-layouts  45.1 us (29%)
  other arithmetic  45 us (29%)
  blocking collectives  40.1 us (26%)
  matrix products  21.1 us (14%)
  starting transfers between devices  3.33 us (2%)
    all_to_all x1, blocking collectives, local(): lax.all_to_all(outgoing, ('inp', 'tim'), split_axis=0, concat_axis=0, til...  40.1 us
    convert_element_type x1, other arithmetic, local(): summed.astype(jnp.bfloat16).reshape(local_inputs * local_frames, NFFT)  19.2 us
    unnamed x6, local copies, waits for them, and re-layouts  14.5 us
    concatenate x1, other arithmetic, local(): jnp.concatenate([voltages, trailing], axis=1)  11.5 us
    reshape x1, local copies, waits for them, and re-layouts, local(): jnp.concatenate([voltages, trailing], axis=1)  9.52 us
    another operation x1, other arithmetic  9.06 us
    another operation x1, local copies, waits for them, and re-layouts, local(): jnp.stack([(real_real + imag_imag) * scale, (imag_real - real_imag) * sca...  6.25 us
    dot_general x1, matrix products, local(): jnp.einsum(form, real_part, imag_part, preferred_element_type=jnp.float32)  5.77 us
  transfers between devices with their start and end apart: 1, of which 0 were waited for; matrix products, arithmetic and copies ran while one was open for 9% of the time, Pallas kernels for 0%

commit v1 on v0

v1 whole, which is shorter than its diff:
```python
import functools
import math

import jax
import jax.numpy as jnp
import numpy as np
from jax import lax
from jax.experimental import pallas as pl
from jax.experimental.pallas import tpu as pltpu
from jax.sharding import PartitionSpec as P

NFFT = 2048
TAPS = 4
CH0 = 384
CHAN = 256
MESH = pl.DeviceIdType.MESH
ROWS = 16
LANES = 128
GROUP = 16
STRIDE = 45


def filter_window():
    span = TAPS * NFFT
    places = np.arange(span).astype(np.float32)
    centred = (places - np.float32(span / 2) + np.float32(0.5)) / np.float32(NFFT)
    taper = 0.5 - 0.5 * np.cos(2.0 * math.pi * (places + 0.5) / span)
    return (np.sinc(centred.astype(np.float64)) * taper).astype(np.float32).reshape(TAPS, NFFT)


def table():
    samples = np.arange(NFFT)
    channels = CH0 + np.arange(CHAN)
    angle = (samples[:, None] * channels[None, :] % NFFT) * (2.0 * math.pi / NFFT)
    both = np.concatenate([np.cos(angle), -np.sin(angle)], axis=1) / math.sqrt(NFFT)
    return both.astype(np.float32).astype(jnp.bfloat16)


def position():
    inp, tim = lax.axis_index("inp"), lax.axis_index("tim")
    return (
        lax.div(inp, 16),
        lax.rem(lax.div(inp, 4), 4),
        lax.rem(inp, 4),
        lax.div(tim, 2),
        lax.rem(tim, 2),
    )


SIZES = (2, 4, 4, 2, 2)


def moved(place, by):
    z_lo, x, y, z_hi, core = [lax.rem(p + b, s) for p, b, s in zip(place, by, SIZES)]
    return z_lo * 16 + x * 4 + y, z_hi * 2 + core


AXES = {"x": 1, "y": 2, "z": 0}


def partners(axis):
    if axis == "tim":
        return [(0, 0, 0, a, b) for a in range(2) for b in range(2) if a or b]
    k = AXES[axis]
    return [tuple(s if q == k else 0 for q in range(5)) for s in range(1, SIZES[k])]


def spread(frames, v_hbm, w_ref, t_ref, recv, vbuf, filt, spec, turned, send,
           load_sem, halo_ssem, halo_rsem, ssem, rsem, stage_sem):
    inp, tim = lax.axis_index("inp"), lax.axis_index("tim")
    place = position()
    span = frames * NFFT
    halo = (TAPS - 1) * NFFT
    groups = frames // GROUP

    def load(half, g):
        cut = pl.ds(g * GROUP * NFFT, GROUP * NFFT)
        return pltpu.make_async_copy(
            v_hbm.at[pl.ds(half * ROWS, ROWS), cut], vbuf.at[half, :, cut], load_sem.at[half, g]
        )

    for half in range(2):
        for g in range(groups):
            load(half, g).start()

    barrier = pltpu.get_barrier_semaphore()
    near = [by for axis in ("tim", "x", "y", "z") for by in partners(axis)]
    for by in near:
        pl.semaphore_signal(barrier, inc=1, device_id=moved(place, by), device_id_type=MESH)

    def halo_copy(half):
        return pltpu.make_async_remote_copy(
            src_ref=v_hbm.at[pl.ds(half * ROWS, ROWS), pl.ds(0, halo)],
            dst_ref=vbuf.at[half, :, pl.ds(span, halo)],
            send_sem=halo_ssem.at[half],
            recv_sem=halo_rsem.at[half],
            device_id=(inp, lax.rem(tim + 3, 4)),
            device_id_type=MESH,
        )

    def filter_group(half, g):
        def lane_tile(j, carry):
            w = [w_ref[t, :, pl.ds(pl.multiple_of(j * LANES, LANES), LANES)] for t in range(TAPS)]

            def frame(f):
                at = pl.multiple_of(f * NFFT + j * LANES, LANES)
                return vbuf[half, :, pl.ds(at, LANES)].astype(jnp.float32)

            held = [frame(g * GROUP + t) for t in range(TAPS - 1)]
            for k in range(GROUP):
                held.append(frame(g * GROUP + k + TAPS - 1))
                total = (w[0] * held[k] + w[1] * held[k + 1]) + (w[2] * held[k + 2] + w[3] * held[k + 3])
                filt[pl.ds(g * GROUP * ROWS + k * ROWS, ROWS), pl.ds(pl.multiple_of(j * LANES, LANES), LANES)] = (
                    total.astype(jnp.bfloat16)
                )
            return carry

        lax.fori_loop(0, NFFT // LANES, lane_tile, 0)

    def transform_group(g):
        rows = pl.ds(g * GROUP * ROWS, GROUP * ROWS)
        found = jnp.dot(filt[rows, :], t_ref[...], preferred_element_type=jnp.float32)
        for q in range(2 * CHAN // LANES):
            spec[q, rows, :] = found[:, q * LANES : (q + 1) * LANES]

    def turn():
        def one(i, carry):
            for block in range(CHAN // LANES):
                parts = [
                    spec[part * (CHAN // LANES) + block, pl.ds(i, frames, stride=ROWS), :]
                    for part in range(2)
                ]
                both = jnp.concatenate(parts, axis=0)
                turned[pl.ds(pl.multiple_of(i * CHAN + block * LANES, LANES), LANES), :] = both.T
            return carry

        lax.fori_loop(0, ROWS, one, 0)

    def slot(ref, half):
        return ref.at[:, tim, pl.ds(pl.multiple_of(inp * 32 + half * ROWS, ROWS), ROWS), :]

    def block_for(to_inp, to_tim, ch):
        c = (to_inp * 4 + to_tim) * 2 + ch
        return turned[pl.ds(c, ROWS, stride=CHAN), :].astype(jnp.bfloat16)

    def send_half(half):
        for ch in range(2):
            recv[ch, tim, pl.ds(pl.multiple_of(inp * 32 + half * ROWS, ROWS), ROWS), :] = block_for(inp, tim, ch)

        def one(r, carry):
            p = lax.rem(r * STRIDE, 128)
            by = (lax.rem(lax.div(p, 16), 2), lax.rem(p, 4), lax.rem(lax.div(p, 4), 4),
                  lax.rem(lax.div(p, 32), 2), lax.div(p, 64))
            to_inp, to_tim = moved(place, by)
            for ch in range(2):
                send[half, r - 1, ch] = block_for(to_inp, to_tim, ch)
            pltpu.make_async_remote_copy(
                src_ref=send.at[half, r - 1],
                dst_ref=slot(recv, half),
                send_sem=ssem,
                recv_sem=rsem,
                device_id=(to_inp, to_tim),
                device_id_type=MESH,
            ).start()
            return carry

        lax.fori_loop(1, 128, one, 0)

    def stage(n, axis):
        group = partners(axis)
        for by in group:
            pl.semaphore_signal(stage_sem.at[n], inc=1, device_id=moved(place, by), device_id_type=MESH)
        pl.semaphore_wait(stage_sem.at[n], len(group))

    for half in range(2):
        for g in range(groups - 1):
            if g == 0:
                load(half, 0).wait()
            load(half, g + 1).wait()
            filter_group(half, g)
            transform_group(g)
            if half == 0:
                if g == 0:
                    pl.semaphore_wait(barrier, len(near))

                    @pl.when(tim > 0)
                    def _():
                        halo_copy(0).start()
                        halo_copy(1).start()

                    stage(0, "x")
                elif g == 1:
                    stage(1, "y")
                elif g == 2:
                    stage(2, "z")

        @pl.when(tim < 3)
        def _():
            halo_copy(half).wait_recv()

        @pl.when(tim == 3)
        def _():
            vbuf[half, :, pl.ds(span, halo)] = jnp.zeros((ROWS, halo), jnp.bfloat16)

        filter_group(half, groups - 1)
        transform_group(groups - 1)
        turn()
        if half == 0:
            stage(3, "tim")
        send_half(half)

    @pl.when(tim > 0)
    def _():
        halo_copy(0).wait_send()
        halo_copy(1).wait_send()

    everything = send.at[:, pl.ds(0, 127)]
    pltpu.make_async_copy(everything, everything, ssem).wait()
    pltpu.make_async_copy(everything, everything, rsem).wait()


def channelize(voltages, window, tab):
    inputs, samples = voltages.shape
    frames = samples // NFFT
    groups = frames // GROUP
    vmem = pl.BlockSpec(memory_space=pltpu.VMEM)
    return pl.pallas_call(
        functools.partial(spread, frames),
        out_shape=jax.ShapeDtypeStruct((2, 4, 1024, LANES), jnp.bfloat16),
        in_specs=[pl.BlockSpec(memory_space=pl.ANY), vmem, vmem],
        out_specs=vmem,
        scratch_shapes=[
            pltpu.VMEM((2, ROWS, samples + (TAPS - 1) * NFFT), jnp.bfloat16),
            pltpu.VMEM((frames * ROWS, NFFT), jnp.bfloat16),
            pltpu.VMEM((2 * CHAN // LANES, frames * ROWS, LANES), jnp.float32),
            pltpu.VMEM((ROWS * CHAN, LANES), jnp.float32),
            pltpu.VMEM((2, 128, 2, ROWS, LANES), jnp.bfloat16),
            pltpu.SemaphoreType.DMA((2, groups)),
            pltpu.SemaphoreType.DMA((2,)),
            pltpu.SemaphoreType.DMA((2,)),
            pltpu.SemaphoreType.DMA,
            pltpu.SemaphoreType.DMA,
            pltpu.SemaphoreType.REGULAR((4,)),
        ],
        compiler_params=pltpu.CompilerParams(
            collective_id=0, has_side_effects=True, vmem_limit_bytes=50 << 20
        ),
        name="channelize",
    )(voltages, window, tab)


def correlate_kernel(scale, rows, x_ref, o_ref):
    step = pl.program_id(1)
    own = pl.ds(pl.multiple_of(step * rows, rows), rows)
    every = jnp.concatenate([x_ref[0, b] for b in range(4)], axis=1)
    mine = [x_ref[0, b, own, :] for b in range(4)]
    half = LANES // 2
    turned = [jnp.concatenate([m[:, half:], -m[:, :half]], axis=1) for m in mine]
    dims = (((1,), (1,)), ((), ()))
    for part, lhs in enumerate((mine, turned)):
        o_ref[0, part] = scale * lax.dot_general(
            jnp.concatenate(lhs, axis=1), every, dims, preferred_element_type=jnp.float32
        )


def correlate(x, scale):
    channels, blocks, inputs, lanes = x.shape
    rows = 256
    return pl.pallas_call(
        functools.partial(correlate_kernel, scale, rows),
        grid=(channels, inputs // rows),
        out_shape=jax.ShapeDtypeStruct((channels, 2, inputs, inputs), jnp.float32),
        in_specs=[pl.BlockSpec((1, blocks, inputs, lanes), lambda c, i: (c, 0, 0, 0))],
        out_specs=pl.BlockSpec((1, 2, rows, inputs), lambda c, i: (c, 0, i, 0)),
        compiler_params=pltpu.CompilerParams(vmem_limit_bytes=40 << 20),
        name="correlate",
    )(x)


def local(voltages):
    frames = voltages.shape[1] // NFFT
    window = np.broadcast_to(filter_window()[:, None, :], (TAPS, ROWS, NFFT))
    received = channelize(voltages, jnp.asarray(window), jnp.asarray(table()))
    return correlate(received, 1.0 / (frames * lax.axis_size("tim")))


def solution(mesh):
    return jax.shard_map(
        local,
        mesh=mesh,
        in_specs=(P("inp", "tim"),),
        out_specs=P(("inp", "tim"), None, None, None),
        check_vma=False,
    )
```

time: 155 us -> 61.9 us (0.40)
  Pallas kernels: 0 us -> 60.9 us
  other arithmetic: 45 us -> 0 us
  local copies, waits for them, and re-layouts: 45.1 us -> 0.79 us
  blocking collectives: 40.1 us -> 0 us
  matrix products: 21.1 us -> 0 us
  starting transfers between devices: 3.33 us -> 0 us
    pallas_call x0 -> x2, Pallas kernels: none -> 60.9 us  [the longest x1 51.8 us: channelize(): pl.pallas_call(functools.partial(spread, frames), out_shape=jax.ShapeDtyp...]
    all_to_all x1 -> x0, blocking collectives: 40.1 us -> none  [local(): lax.all_to_all(outgoing, ('inp', 'tim'), split_axis=0, concat_axis=0, til...]
    dot_general x5 -> x0, matrix products: 21.1 us -> none  [the longest x1 5.77 us: local(): jnp.einsum(form, real_part, imag_part, preferred_element_type=jnp.float32)]
    convert_element_type x1 -> x0, other arithmetic: 19.2 us -> none  [local(): summed.astype(jnp.bfloat16).reshape(local_inputs * local_frames, NFFT)]
    reshape x3 -> x0, local copies, waits for them, and re-layouts: 18.1 us -> none  [the longest x1 9.52 us: local(): jnp.concatenate([voltages, trailing], axis=1)]
    unnamed x6 -> x0, local copies, waits for them, and re-layouts: 14.5 us -> none
    another operation x2 -> x0, other arithmetic: 13.9 us -> none
    concatenate x2 -> x0, other arithmetic: 11.7 us -> none  [the longest x1 11.5 us: local(): jnp.concatenate([voltages, trailing], axis=1)]
  transfers between devices with their start and end apart: 1 -> 0, of which waited for: 0 -> 0; matrix products, arithmetic and copies ran while one was open for 9% -> 0% of each run, Pallas kernels for 0% -> 0%
where the time goes in v1:
time: 61.9 us; the launch traced here: 61.7 us
  Pallas kernels  60.9 us (98%)
  local copies, waits for them, and re-layouts  0.79 us (1%)
    pallas_call x1, Pallas kernels, channelize(): pl.pallas_call(functools.partial(spread, frames), out_shape=jax.ShapeDtyp...  51.8 us
    pallas_call x1, Pallas kernels, correlate(): pl.pallas_call(functools.partial(correlate_kernel, scale, rows), grid=(ch...  9.05 us

profile of v1, /device:TPU:1, one launch (start us, length us, event | category | flops | bytes accessed | tf_op | source)
XLA Modules:
  0.0 61.7 jit_solution(4209332441590213934)
XLA Ops:
  0.0 0.8 %jit_solution_.3.w_ref = f32[4,16,2048]{2,1,0:T(8,128)S(1)} broadcast(f32[4,2048]{1,0:T(4,128)} %constant.4.clone), dimensions={0,2} | broadcast | bytes 557056 | tf_op jit(solution)
  0.8 51.8 %channelize.1.x_ref = bf16[2,4,1024,128]{3,2,1,0:T(8,128)(2,1)S(1)} custom-call(bf16[32,131072]{1,0:T(8,128)(2,1)} %v_hbm.1, f32[4,16,2048]{2,1,0:T(8,128)S(1)} %jit_solution_.3.w_ref, bf16[2048,512]{1,0:T(8,128)(2,1)} %constant.5.clone.t_ref), custom_call_target="tpu_custom_call" | custom-call | tf_op jit(solution)/shard_map/channelize/pallas_call | solution.py:227
  52.6 9.1 %correlate.1 = f32[2,2,1024,1024]{3,2,1,0:T(8,128)} custom-call(bf16[2,4,1024,128]{3,2,1,0:T(8,128)(2,1)S(1)} %channelize.1.x_ref), custom_call_target="tpu_custom_call" | custom-call | tf_op jit(solution)/shard_map/correlate/pallas_call | solution.py:269

commit v2 on v1

v2 whole, which is shorter than its diff:
```python
import functools
import math

import jax
import jax.numpy as jnp
import numpy as np
from jax import lax
from jax.experimental import pallas as pl
from jax.experimental.pallas import tpu as pltpu
from jax.sharding import PartitionSpec as P

NFFT = 2048
TAPS = 4
CH0 = 384
CHAN = 256
MESH = pl.DeviceIdType.MESH
ROWS = 16
LANES = 128
GROUP = 16
STRIDE = 85
PITCH = 65
LEAD = 257
CORR_ROWS = 256


def filter_window():
    span = TAPS * NFFT
    places = np.arange(span).astype(np.float32)
    centred = (places - np.float32(span / 2) + np.float32(0.5)) / np.float32(NFFT)
    taper = 0.5 - 0.5 * np.cos(2.0 * math.pi * (places + 0.5) / span)
    return (np.sinc(centred.astype(np.float64)) * taper).astype(np.float32).reshape(TAPS, NFFT)


def table():
    samples = np.arange(NFFT)
    channels = CH0 + np.arange(CHAN)
    angle = (samples[:, None] * channels[None, :] % NFFT) * (2.0 * math.pi / NFFT)
    both = np.concatenate([np.cos(angle), -np.sin(angle)], axis=1) / math.sqrt(NFFT)
    return both.astype(np.float32).astype(jnp.bfloat16)


def position():
    inp, tim = lax.axis_index("inp"), lax.axis_index("tim")
    return (
        lax.div(inp, 16),
        lax.rem(lax.div(inp, 4), 4),
        lax.rem(inp, 4),
        lax.div(tim, 2),
        lax.rem(tim, 2),
    )


SIZES = (2, 4, 4, 2, 2)


def moved(place, by):
    z_lo, x, y, z_hi, core = [lax.rem(p + b, s) for p, b, s in zip(place, by, SIZES)]
    return z_lo * 16 + x * 4 + y, z_hi * 2 + core


def partners(axis):
    if axis == "column":
        return [(a, 0, 0, b, c) for a in range(2) for b in range(2) for c in range(2) if a or b or c]
    k = {"x": 1, "y": 2}[axis]
    return [tuple(s if q == k else 0 for q in range(5)) for s in range(1, 4)]


def spread(frames, v_hbm, w_hbm, t_hbm, recv, vbuf, w_ref, t_ref, filt, spec, turned, send,
           load_sem, const_sem, halo_ssem, halo_rsem, own_sem, ssem, rsem, stage_sem):
    inp, tim = lax.axis_index("inp"), lax.axis_index("tim")
    me = inp * 4 + tim
    place = position()
    span = frames * NFFT
    halo = (TAPS - 1) * NFFT
    groups = frames // GROUP

    def load(half, g):
        cut = pl.ds(g * GROUP * NFFT, GROUP * NFFT)
        return pltpu.make_async_copy(
            v_hbm.at[pl.ds(half * ROWS, ROWS), cut], vbuf.at[half, :, cut], load_sem.at[half, g]
        )

    load_w = pltpu.make_async_copy(w_hbm, w_ref, const_sem.at[0])
    load_t = pltpu.make_async_copy(t_hbm, t_ref, const_sem.at[1])
    load_w.start()
    for g in range(groups):
        load(0, g).start()
        if g == 1:
            load_t.start()

    barrier = pltpu.get_barrier_semaphore()
    near = [by for axis in ("column", "x", "y") for by in partners(axis)]
    for by in near:
        pl.semaphore_signal(barrier, inc=1, device_id=moved(place, by), device_id_type=MESH)

    def halo_copy(half):
        return pltpu.make_async_remote_copy(
            src_ref=v_hbm.at[pl.ds(half * ROWS, ROWS), pl.ds(0, halo)],
            dst_ref=vbuf.at[half, :, pl.ds(span, halo)],
            send_sem=halo_ssem.at[half],
            recv_sem=halo_rsem.at[half],
            device_id=(inp, lax.rem(tim + 3, 4)),
            device_id_type=MESH,
        )

    tiles = NFFT // LANES // 2

    def filter_group(half, g, side):
        for j in range(tiles):
            lane = pl.multiple_of((side * tiles + j) * LANES, LANES)
            w = [jnp.broadcast_to(w_ref[pl.ds(t, 1), pl.ds(lane, LANES)], (ROWS, LANES)) for t in range(TAPS)]

            def frame(f):
                at = pl.multiple_of((g * GROUP + f) * NFFT + lane, LANES)
                return vbuf[half, :, pl.ds(at, LANES)].astype(jnp.float32)

            held = [frame(t) for t in range(TAPS - 1)]
            for k in range(GROUP):
                held.append(frame(k + TAPS - 1))
                total = (w[0] * held[k] + w[1] * held[k + 1]) + (w[2] * held[k + 2] + w[3] * held[k + 3])
                rows = pl.ds(pl.multiple_of((g * GROUP + k) * ROWS, ROWS), ROWS)
                filt[rows, pl.ds(lane, LANES)] = total.astype(jnp.bfloat16)

    def product(g, side):
        rows = pl.ds(pl.multiple_of(g * GROUP * ROWS, GROUP * ROWS), GROUP * ROWS)
        cut = pl.ds(pl.multiple_of(side * CHAN, CHAN), CHAN)
        return jnp.dot(filt[rows, :], t_ref[:, cut], preferred_element_type=jnp.float32)

    def keep(g, side, found):
        for q in range(CHAN // LANES):
            for k in range(GROUP):
                for h in range(ROWS // 8):
                    at = h * 8 * PITCH + g * GROUP + k
                    spec[side * 2 + q, pl.ds(at, 8, stride=PITCH), :] = found[
                        k * ROWS + h * 8 : k * ROWS + h * 8 + 8, q * LANES : (q + 1) * LANES
                    ]

    def front(half, g, with_filter, with_product):
        def one(side, carry):
            if with_product:
                found = product(g - 1, side)
            if with_filter:
                filter_group(half, g, side)
            if with_product:
                keep(g - 1, side, found)
            return carry

        lax.fori_loop(0, 2, one, 0)

    def turn():
        def one(n, carry):
            for i in (n * 2, n * 2 + 1):
                for block in range(CHAN // LANES):
                    both = jnp.concatenate(
                        [spec[part * 2 + block, pl.ds(i * PITCH, frames), :] for part in range(2)], axis=0
                    )
                    turned[pl.ds(i * LEAD + block * LANES, LANES), :] = both.astype(jnp.bfloat16).T.astype(jnp.float32)
            return carry

        lax.fori_loop(0, ROWS // 2, one, 0)

    def pack(half):
        def one(n, carry):
            for k in range(4):
                for ch in range(2):
                    c = n * 8 + k * 2 + ch
                    send[half, n * 4 + k, ch] = turned[pl.ds(c, ROWS, stride=LEAD), :].astype(jnp.bfloat16)
            return carry

        lax.fori_loop(0, CHAN // 8, one, 0)

    def slot(half):
        return recv.at[:, tim, pl.ds(pl.multiple_of(inp * 32 + half * ROWS, ROWS), ROWS), :]

    def own_copy(half):
        return pltpu.make_async_copy(send.at[half, me], slot(half), own_sem.at[half])

    def send_to(half, r):
        p = lax.rem(r * STRIDE, 128)
        by = (lax.rem(lax.div(p, 16), 2), lax.rem(p, 4), lax.rem(lax.div(p, 4), 4),
              lax.rem(lax.div(p, 32), 2), lax.div(p, 64))
        to_inp, to_tim = moved(place, by)
        pltpu.make_async_remote_copy(
            src_ref=send.at[half, to_inp * 4 + to_tim],
            dst_ref=slot(half),
            send_sem=ssem,
            recv_sem=rsem,
            device_id=(to_inp, to_tim),
            device_id_type=MESH,
        ).start()

    def send_half(half):
        own_copy(half).start()

        def one(n, carry):
            for k in range(7):
                send_to(half, 1 + n * 7 + k)
            return carry

        lax.fori_loop(0, 18, one, 0)
        send_to(half, 127)

    def stage(n, axis):
        group = partners(axis)
        for by in group:
            pl.semaphore_signal(stage_sem.at[n], inc=1, device_id=moved(place, by), device_id_type=MESH)
        pl.semaphore_wait(stage_sem.at[n], len(group))

    for half in range(2):
        load(half, 0).wait()
        load(half, 1).wait()
        if half == 0:
            for g in range(groups):
                load(1, g).start()
            load_w.wait()
        front(half, 0, True, False)
        if half == 0:
            load_t.wait()
            pl.semaphore_wait(barrier, len(near))

            @pl.when(tim > 0)
            def _():
                halo_copy(0).start()
                halo_copy(1).start()

        load(half, 2).wait()
        front(half, 1, True, True)
        if half == 0:
            stage(0, "x")
        load(half, 3).wait()
        front(half, 2, True, True)

        @pl.when(tim < 3)
        def _():
            halo_copy(half).wait_recv()

        @pl.when(tim == 3)
        def _():
            vbuf[half, :, pl.ds(span, halo)] = jnp.zeros((ROWS, halo), jnp.bfloat16)

        front(half, 3, True, True)
        front(half, 4, False, True)
        turn()
        pack(half)
        if half == 0:
            stage(1, "y")
        send_half(half)

    @pl.when(tim > 0)
    def _():
        halo_copy(0).wait_send()
        halo_copy(1).wait_send()

    own_copy(0).wait()
    own_copy(1).wait()
    everything = send.at[:, pl.ds(0, 127)]
    pltpu.make_async_copy(everything, everything, ssem).wait()
    pltpu.make_async_copy(everything, everything, rsem).wait()


def channelize(voltages, window, tab):
    samples = voltages.shape[1]
    frames = samples // NFFT
    groups = frames // GROUP
    hbm = pl.BlockSpec(memory_space=pltpu.HBM)
    return pl.pallas_call(
        functools.partial(spread, frames),
        out_shape=jax.ShapeDtypeStruct((2, 4, 1024, LANES), jnp.bfloat16),
        in_specs=[hbm, hbm, hbm],
        out_specs=pl.BlockSpec(memory_space=pltpu.VMEM),
        scratch_shapes=[
            pltpu.VMEM((2, ROWS, samples + (TAPS - 1) * NFFT), jnp.bfloat16),
            pltpu.VMEM((TAPS, NFFT), jnp.float32),
            pltpu.VMEM((NFFT, 2 * CHAN), jnp.bfloat16),
            pltpu.VMEM((frames * ROWS, NFFT), jnp.bfloat16),
            pltpu.VMEM((2 * CHAN // LANES, ROWS * PITCH + 72, LANES), jnp.float32),
            pltpu.VMEM((ROWS * LEAD + 264, LANES), jnp.float32),
            pltpu.VMEM((2, 128, 2, ROWS, LANES), jnp.bfloat16),
            pltpu.SemaphoreType.DMA((2, groups)),
            pltpu.SemaphoreType.DMA((2,)),
            pltpu.SemaphoreType.DMA((2,)),
            pltpu.SemaphoreType.DMA((2,)),
            pltpu.SemaphoreType.DMA((2,)),
            pltpu.SemaphoreType.DMA,
            pltpu.SemaphoreType.DMA,
            pltpu.SemaphoreType.REGULAR((2,)),
        ],
        compiler_params=pltpu.CompilerParams(
            collective_id=0, has_side_effects=True, vmem_limit_bytes=50 << 20
        ),
        name="channelize",
    )(voltages, window, tab)


def correlate_kernel(scale, rows, x_ref, o_hbm, obuf, sem):
    channels, blocks, inputs, lanes = x_ref.shape
    half = lanes // 2
    dims = (((1,), (1,)), ((), ()))

    def copy(ch, n):
        own = pl.ds(n * rows, rows)
        return pltpu.make_async_copy(obuf.at[ch, :, own, :], o_hbm.at[ch, :, own, :], sem.at[ch, n])

    for ch in range(channels):
        for n in range(inputs // rows):
            every = jnp.concatenate([x_ref[ch, b] for b in range(blocks)], axis=1)
            own = pl.ds(n * rows, rows)
            mine = [x_ref[ch, b, own, :] for b in range(blocks)]
            swapped = [jnp.concatenate([m[:, half:], -m[:, :half]], axis=1) for m in mine]
            for part, lhs in enumerate((mine, swapped)):
                obuf[ch, part, own, :] = scale * lax.dot_general(
                    jnp.concatenate(lhs, axis=1), every, dims, preferred_element_type=jnp.float32
                )
            copy(ch, n).start()
    for ch in range(channels):
        for n in range(inputs // rows):
            copy(ch, n).wait()


def correlate(x, scale):
    channels, blocks, inputs, lanes = x.shape
    rows = CORR_ROWS
    shape = (channels, 2, inputs, inputs)
    return pl.pallas_call(
        functools.partial(correlate_kernel, scale, rows),
        out_shape=jax.ShapeDtypeStruct(shape, jnp.float32),
        in_specs=[pl.BlockSpec(memory_space=pltpu.VMEM)],
        out_specs=pl.BlockSpec(memory_space=pl.ANY),
        scratch_shapes=[
            pltpu.VMEM(shape, jnp.float32),
            pltpu.SemaphoreType.DMA((channels, inputs // rows)),
        ],
        compiler_params=pltpu.CompilerParams(vmem_limit_bytes=40 << 20),
        name="correlate",
    )(x)


def local(voltages):
    frames = voltages.shape[1] // NFFT
    received = channelize(voltages, jnp.asarray(filter_window()), jnp.asarray(table()))
    return correlate(received, 1.0 / (frames * lax.axis_size("tim")))


def solution(mesh):
    return jax.shard_map(
        local,
        mesh=mesh,
        in_specs=(P("inp", "tim"),),
        out_specs=P(("inp", "tim"), None, None, None),
        check_vma=False,
    )
```

time: 61.9 us -> 50.5 us (0.82)
  Pallas kernels: 60.9 us -> 49.6 us
    pallas_call x1, Pallas kernels: 51.8 us -> 42.9 us  [channelize(): pl.pallas_call(functools.partial(spread, frames), out_shape=jax.ShapeDtyp...]
    pallas_call x1, Pallas kernels: 9.05 us -> 6.66 us  [correlate(): pl.pallas_call(functools.partial(correlate_kernel, scale, rows), out_shap...]
    another operation x1 -> x0, local copies, waits for them, and re-layouts: 0.79 us -> none
    unnamed x0 -> x2, local copies, waits for them, and re-layouts: none -> 0.76 us
where the time goes in v2:
time: 50.5 us; the launch traced here: 50.3 us
  Pallas kernels  49.6 us (98%)
  local copies, waits for them, and re-layouts  0.76 us (2%)
    pallas_call x1, Pallas kernels, channelize(): pl.pallas_call(functools.partial(spread, frames), out_shape=jax.ShapeDtyp...  42.9 us
    pallas_call x1, Pallas kernels, correlate(): pl.pallas_call(functools.partial(correlate_kernel, scale, rows), out_shap...  6.66 us

profile of v2, /device:TPU:1, one launch (start us, length us, event | category | flops | bytes accessed | tf_op | source)
XLA Modules:
  0.0 50.3 jit_solution(18342533128139054901)
XLA Ops:
  0.0 0.0 copy-start
  0.0 0.8 %copy-done = f32[4,2048]{1,0:T(4,128)S(1)} copy-done((f32[4,2048]{1,0:T(4,128)S(1)}, f32[4,2048]{1,0:T(4,128)}, u32[]{:S(2)}) %copy-start) | copy-done | bytes 32792
  0.8 42.9 %channelize.1.x_ref = bf16[2,4,1024,128]{3,2,1,0:T(8,128)(2,1)S(1)} custom-call(bf16[32,131072]{1,0:T(8,128)(2,1)} %v_hbm.1, f32[4,2048]{1,0:T(4,128)S(1)} %copy-done, bf16[2048,512]{1,0:T(8,128)(2,1)} %constant.5.clone.t_hbm), custom_call_target="tpu_custom_call" | custom-call | tf_op jit(solution)/shard_map/channelize/pallas_call | solution.py:266
  43.7 6.7 %correlate.1 = f32[2,2,1024,1024]{3,2,1,0:T(8,128)} custom-call(bf16[2,4,1024,128]{3,2,1,0:T(8,128)(2,1)S(1)} %channelize.1.x_ref), custom_call_target="tpu_custom_call" | custom-call | tf_op jit(solution)/shard_map/correlate/pallas_call | solution.py:324
Async XLA Ops:
  0.0 0.8 %copy-start = (f32[4,2048]{1,0:T(4,128)S(1)}, f32[4,2048]{1,0:T(4,128)}, u32[]{:S(2)}) copy-start(f32[4,2048]{1,0:T(4,128)} %constant.4.clone.w_hbm) | copy-start | bytes 98308

commit v3 on v2

--- a/solution.py
+++ b/solution.py
@@ -21,6 +21,7 @@
 PITCH = 65
 LEAD = 257
 CORR_ROWS = 256
+WINDOW_ROWS = 3 * TAPS * NFFT // (2 * CHAN)
 
 
 def filter_window():
@@ -36,7 +37,12 @@
     channels = CH0 + np.arange(CHAN)
     angle = (samples[:, None] * channels[None, :] % NFFT) * (2.0 * math.pi / NFFT)
     both = np.concatenate([np.cos(angle), -np.sin(angle)], axis=1) / math.sqrt(NFFT)
-    return both.astype(np.float32).astype(jnp.bfloat16)
+    rest, terms = filter_window(), []
+    for _ in range(3):
+        terms.append(rest.astype(jnp.bfloat16))
+        rest = rest - terms[-1].astype(np.float32)
+    terms = np.stack(terms).reshape(WINDOW_ROWS, 2 * CHAN)
+    return np.concatenate([both.astype(np.float32).astype(jnp.bfloat16), terms], axis=0)
 
 
 def position():
@@ -65,7 +71,7 @@
     return [tuple(s if q == k else 0 for q in range(5)) for s in range(1, 4)]
 
 
-def spread(frames, v_hbm, w_hbm, t_hbm, recv, vbuf, w_ref, t_ref, filt, spec, turned, send,
+def spread(frames, v_hbm, t_hbm, recv, vbuf, w_ref, wt_ref, t_ref, filt, spec, turned, send,
            load_sem, const_sem, halo_ssem, halo_rsem, own_sem, ssem, rsem, stage_sem):
     inp, tim = lax.axis_index("inp"), lax.axis_index("tim")
     me = inp * 4 + tim
@@ -75,17 +81,19 @@
     groups = frames // GROUP
 
     def load(half, g):
-        cut = pl.ds(g * GROUP * NFFT, GROUP * NFFT)
+        first = g * GROUP + (TAPS - 1 if g else 0)
+        last = (g + 1) * GROUP + TAPS - 1 if g < groups - 1 else frames
+        cut = pl.ds(first * NFFT, (last - first) * NFFT)
         return pltpu.make_async_copy(
             v_hbm.at[pl.ds(half * ROWS, ROWS), cut], vbuf.at[half, :, cut], load_sem.at[half, g]
         )
 
-    load_w = pltpu.make_async_copy(w_hbm, w_ref, const_sem.at[0])
-    load_t = pltpu.make_async_copy(t_hbm, t_ref, const_sem.at[1])
+    load_w = pltpu.make_async_copy(t_hbm.at[pl.ds(NFFT, WINDOW_ROWS)], wt_ref, const_sem.at[0])
+    load_t = pltpu.make_async_copy(t_hbm.at[pl.ds(0, NFFT)], t_ref, const_sem.at[1])
     load_w.start()
     for g in range(groups):
         load(0, g).start()
-        if g == 1:
+        if g == 0:
             load_t.start()
 
     barrier = pltpu.get_barrier_semaphore()
@@ -105,6 +113,13 @@
 
     tiles = NFFT // LANES // 2
 
+    def window():
+        per = NFFT // (2 * CHAN)
+        for t in range(TAPS):
+            for q in range(per):
+                terms = [wt_ref[pl.ds((k * TAPS + t) * per + q, 1), :].astype(jnp.float32) for k in range(3)]
+                w_ref[pl.ds(t, 1), pl.ds(q * 2 * CHAN, 2 * CHAN)] = (terms[0] + terms[1]) + terms[2]
+
     def filter_group(half, g, side):
         for j in range(tiles):
             lane = pl.multiple_of((side * tiles + j) * LANES, LANES)
@@ -170,7 +185,7 @@
         lax.fori_loop(0, CHAN // 8, one, 0)
 
     def slot(half):
-        return recv.at[:, tim, pl.ds(pl.multiple_of(inp * 32 + half * ROWS, ROWS), ROWS), :]
+        return recv.at[tim, inp, half]
 
     def own_copy(half):
         return pltpu.make_async_copy(send.at[half, me], slot(half), own_sem.at[half])
@@ -200,21 +215,22 @@
         lax.fori_loop(0, 18, one, 0)
         send_to(half, 127)
 
-    def stage(n, axis):
-        group = partners(axis)
-        for by in group:
+    def tell(n, axis):
+        for by in partners(axis):
             pl.semaphore_signal(stage_sem.at[n], inc=1, device_id=moved(place, by), device_id_type=MESH)
-        pl.semaphore_wait(stage_sem.at[n], len(group))
+
+    def hear(n, axis):
+        pl.semaphore_wait(stage_sem.at[n], len(partners(axis)))
 
     for half in range(2):
+        if half == 0:
+            load_w.wait()
+            window()
         load(half, 0).wait()
-        load(half, 1).wait()
+        front(half, 0, True, False)
         if half == 0:
             for g in range(groups):
                 load(1, g).start()
-            load_w.wait()
-        front(half, 0, True, False)
-        if half == 0:
             load_t.wait()
             pl.semaphore_wait(barrier, len(near))
 
@@ -223,12 +239,15 @@
                 halo_copy(0).start()
                 halo_copy(1).start()
 
+            tell(0, "x")
+        load(half, 1).wait()
+        front(half, 1, True, True)
         load(half, 2).wait()
-        front(half, 1, True, True)
+        front(half, 2, True, True)
+        load(half, 3).wait()
         if half == 0:
-            stage(0, "x")
-        load(half, 3).wait()
-        front(half, 2, True, True)
+            hear(0, "x")
+            tell(1, "y")
 
         @pl.when(tim < 3)
         def _():
@@ -243,7 +262,7 @@
         turn()
         pack(half)
         if half == 0:
-            stage(1, "y")
+            hear(1, "y")
         send_half(half)
 
     @pl.when(tim > 0)
@@ -258,19 +277,20 @@
     pltpu.make_async_copy(everything, everything, rsem).wait()
 
 
-def channelize(voltages, window, tab):
+def channelize(voltages, tab):
     samples = voltages.shape[1]
     frames = samples // NFFT
     groups = frames // GROUP
     hbm = pl.BlockSpec(memory_space=pltpu.HBM)
     return pl.pallas_call(
         functools.partial(spread, frames),
-        out_shape=jax.ShapeDtypeStruct((2, 4, 1024, LANES), jnp.bfloat16),
-        in_specs=[hbm, hbm, hbm],
+        out_shape=jax.ShapeDtypeStruct((4, 32, 2, 2, ROWS, LANES), jnp.bfloat16),
+        in_specs=[hbm, hbm],
         out_specs=pl.BlockSpec(memory_space=pltpu.VMEM),
         scratch_shapes=[
             pltpu.VMEM((2, ROWS, samples + (TAPS - 1) * NFFT), jnp.bfloat16),
             pltpu.VMEM((TAPS, NFFT), jnp.float32),
+            pltpu.VMEM((WINDOW_ROWS, 2 * CHAN), jnp.bfloat16),
             pltpu.VMEM((NFFT, 2 * CHAN), jnp.bfloat16),
             pltpu.VMEM((frames * ROWS, NFFT), jnp.bfloat16),
             pltpu.VMEM((2 * CHAN // LANES, ROWS * PITCH + 72, LANES), jnp.float32),
@@ -289,12 +309,14 @@
             collective_id=0, has_side_effects=True, vmem_limit_bytes=50 << 20
         ),
         name="channelize",
-    )(voltages, window, tab)
+    )(voltages, tab)
 
 
 def correlate_kernel(scale, rows, x_ref, o_hbm, obuf, sem):
-    channels, blocks, inputs, lanes = x_ref.shape
+    blocks, sources, halves, channels, _, lanes = x_ref.shape
+    inputs = o_hbm.shape[-1]
     half = lanes // 2
+    per = inputs // sources
     dims = (((1,), (1,)), ((), ()))
 
     def copy(ch, n):
@@ -303,9 +325,9 @@
 
     for ch in range(channels):
         for n in range(inputs // rows):
-            every = jnp.concatenate([x_ref[ch, b] for b in range(blocks)], axis=1)
+            every = jnp.concatenate([x_ref[b, :, :, ch].reshape(inputs, lanes) for b in range(blocks)], axis=1)
             own = pl.ds(n * rows, rows)
-            mine = [x_ref[ch, b, own, :] for b in range(blocks)]
+            mine = [x_ref[b, pl.ds(n * rows // per, rows // per), :, ch].reshape(rows, lanes) for b in range(blocks)]
             swapped = [jnp.concatenate([m[:, half:], -m[:, :half]], axis=1) for m in mine]
             for part, lhs in enumerate((mine, swapped)):
                 obuf[ch, part, own, :] = scale * lax.dot_general(
@@ -318,7 +340,8 @@
 
 
 def correlate(x, scale):
-    channels, blocks, inputs, lanes = x.shape
+    _, sources, halves, channels, part_rows, _ = x.shape
+    inputs = sources * halves * part_rows
     rows = CORR_ROWS
     shape = (channels, 2, inputs, inputs)
     return pl.pallas_call(
@@ -337,7 +360,7 @@
 
 def local(voltages):
     frames = voltages.shape[1] // NFFT
-    received = channelize(voltages, jnp.asarray(filter_window()), jnp.asarray(table()))
+    received = channelize(voltages, jnp.asarray(table()))
     return correlate(received, 1.0 / (frames * lax.axis_size("tim")))
 
 

time: 50.5 us -> 47 us (0.931)
  Pallas kernels: 49.6 us -> 46.9 us
  local copies, waits for them, and re-layouts: 0.76 us -> 0 us
    pallas_call x1, Pallas kernels: 42.9 us -> 40.2 us  [channelize(): pl.pallas_call(functools.partial(spread, frames), out_shape=jax.ShapeDtyp...]
    unnamed x2 -> x0, local copies, waits for them, and re-layouts: 0.76 us -> none
where the time goes in v3:
time: 47 us; the launch traced here: 46.9 us
  Pallas kernels  46.9 us (100%)
    pallas_call x1, Pallas kernels, channelize(): pl.pallas_call(functools.partial(spread, frames), out_shape=jax.ShapeDtyp...  40.2 us
    pallas_call x1, Pallas kernels, correlate(): pl.pallas_call(functools.partial(correlate_kernel, scale, rows), out_shap...  6.66 us

profile of v3, /device:TPU:1, one launch (start us, length us, event | category | flops | bytes accessed | tf_op | source)
XLA Modules:
  0.0 46.9 jit_solution(1505075859779408958)
XLA Ops:
  0.0 40.2 %channelize.1.x_ref = bf16[4,32,2,2,16,128]{5,4,3,2,1,0:T(8,128)(2,1)S(1)} custom-call(bf16[32,131072]{1,0:T(8,128)(2,1)} %v_hbm.1, bf16[2096,512]{1,0:T(8,128)(2,1)} %constant.2.clone.t_hbm), custom_call_target="tpu_custom_call" | custom-call | tf_op jit(solution)/shard_map/channelize/pallas_call | solution.py:285
  40.2 6.7 %correlate.1 = f32[2,2,1024,1024]{3,2,1,0:T(8,128)} custom-call(bf16[4,32,2,2,16,128]{5,4,3,2,1,0:T(8,128)(2,1)S(1)} %channelize.1.x_ref), custom_call_target="tpu_custom_call" | custom-call | tf_op jit(solution)/shard_map/correlate/pallas_call | solution.py:347
